TPU v7x, 32 devices: a whole 2x2x4 slice. The times are simulated.
32 devices in a mesh: pole: 2 (over y), row: 4 (over z), col: 4 (over x, core).
Axes of the slice: x: 2, y: 2, z: 4, core: 2. Of those that a mesh axis runs over, the one named last changes fastest.
Arguments:
- root_inverse: float32 [16384, 8192], P(('pole', 'row'), 'col'), parts along dimension 0, may hold values from -6 to 6
- lower_one: float32 [16384, 512], P(('pole', 'row'), 'col'), parts along dimension 0, may hold values from -0.0625 to 0.0625
- pattern_one: int32 [64, 4], replicated, may hold values from 0 to 1, as said below
- diag_one: float32 [256, 512], P('pole', 'col'), parts along dimension 0, may hold values from -6 to 6
- lower_two: float32 [16384, 1024], P(('pole', 'row'), 'col'), parts along dimension 0, may hold values from -0.0625 to 0.0625
- pattern_two: int32 [64, 8], replicated, may hold values from 0 to 1, as said below
- parent_two: int32 [8], replicated, may hold values from 0 to 3, as said below
- lower_parent: float32 [256, 1024], P('pole', 'col'), parts along dimension 0, may hold values from -0.5 to 0.5
- diag_two: float32 [256, 1024], P('pole', 'col'), parts along dimension 0, may hold values from -6 to 6
Outputs:
- inverse_off_one: float32 [16384, 512], P(('pole', 'row'), 'col'), parts along dimension 0
- inverse_diagonal_first: float32 [256, 512], P('pole', 'col'), parts along dimension 0
- inverse_off_two: float32 [16384, 1024], P(('pole', 'row'), 'col'), parts along dimension 0
- inverse_parent_two: float32 [256, 1024], P('pole', 'col'), parts along dimension 0
- inverse_diag_two: float32 [256, 1024], P('pole', 'col'), parts along dimension 0
There are 2 independent parts, one for each index of `pole`. A program takes and returns all parts, laid end to end along the dimension named above; an argument that names none is the same for every part. Nothing has to cross between parts.
Inputs may be any that keep to these rules, and one draw needn't show every extreme that they name: pattern_one[i, k] is 1 where root block row i lies in the structure of first-level supernode k. `parent_two`: each first-level supernode is the parent of exactly two second-level supernodes. pattern_two[i, m] is 1 only where pattern_one[i, parent_two[m]] is 1.
All inputs are finite; a program needn't handle non-finite values.
Results may differ from a plain program's by a relative error of at most 0.000088.
Values sent between devices are 32-bit elements; how exact they have to be, the bound alone decides.
A program may use at most 128 MiB of HBM per device.

v0:
```python
import jax
import jax.numpy as jnp
from jax import lax
from jax.sharding import PartitionSpec as P

BLOCK_SIDE = 128


PRECISION_MODE = lax.Precision.HIGHEST


def expand_blocks(pattern, block):
    count_rows, count_cols = pattern.shape
    spread = jnp.broadcast_to(
        pattern.astype(jnp.float32)[:, None, :, None], (count_rows, block, count_cols, block)
    )
    return spread.reshape(count_rows * block, count_cols * block)


def product(left_part, right_part):
    return jnp.dot(
        left_part, right_part, precision=PRECISION_MODE, preferred_element_type=jnp.float32
    )


def guarded(left_part, right_part):
    return product(left_part, right_part)


def block_inner(masked, solved):
    rows_here = masked.shape[0]
    blocks = masked.shape[1] // BLOCK_SIDE
    inner = jnp.einsum(
        "ikb,ikc->bkc",
        masked.reshape(rows_here, blocks, BLOCK_SIDE),
        solved.reshape(rows_here, blocks, BLOCK_SIDE),
        precision=PRECISION_MODE,
    )
    return inner.reshape(BLOCK_SIDE, blocks * BLOCK_SIDE)


def column_sums(partial_sum):
    return lax.psum_scatter(partial_sum, "col", scatter_dimension=1, tiled=True)


def block_totals(stacked):
    return lax.psum(stacked, "row")


def broadcast_product(root_block, masked):
    ranks_row = lax.axis_size("row")
    ranks_col = lax.axis_size("col")
    rows_here = root_block.shape[0]
    piece_width = masked.shape[1] // ranks_row
    swapped = lax.all_to_all(
        lax.all_to_all(masked, "row", split_axis=1, concat_axis=0, tiled=True),
        "col",
        split_axis=0,
        concat_axis=1,
        tiled=True,
    )
    gathered = guarded(root_block, lax.all_gather(swapped, "row", axis=1, tiled=True))
    ordered = gathered.reshape(rows_here, ranks_row, ranks_col, piece_width).transpose(0, 2, 1, 3)
    return ordered.reshape(rows_here, ranks_row * ranks_col * piece_width)


def local(
    root_inverse,
    lower_one,
    pattern_one,
    diag_one,
    lower_two,
    pattern_two,
    parent_two,
    lower_parent,
    diag_two,
):
    rows_here = root_inverse.shape[0]
    row_blocks = rows_here // BLOCK_SIDE
    row_start = lax.axis_index("row") * row_blocks
    col_index = lax.axis_index("col")
    col_one = lower_one.shape[1] // BLOCK_SIDE
    col_two = lower_two.shape[1] // BLOCK_SIDE
    first_supernodes = pattern_one.shape[1]
    super_two = pattern_two.shape[1]
    rows_one = lax.dynamic_slice_in_dim(pattern_one, row_start, row_blocks, 0)
    rows_two = lax.dynamic_slice_in_dim(pattern_two, row_start, row_blocks, 0)
    mask_one = expand_blocks(
        lax.dynamic_slice_in_dim(rows_one, col_index * col_one, col_one, 1), BLOCK_SIDE
    )
    mask_two = expand_blocks(
        lax.dynamic_slice_in_dim(rows_two, col_index * col_two, col_two, 1), BLOCK_SIDE
    )
    masked_one = lower_one * mask_one
    masked_two = lower_two * mask_two
    owned_parent = lax.dynamic_slice_in_dim(parent_two, col_index * col_two, col_two, 0)
    select_owned_blocks = (
        owned_parent[None, :] == jnp.arange(first_supernodes, dtype=jnp.int32)[:, None]
    ).astype(jnp.float32)
    link_own = lower_parent.reshape(BLOCK_SIDE, col_two, BLOCK_SIDE)
    solved_one = column_sums(broadcast_product(root_inverse, masked_one))
    inverse_off_one = -(mask_one * solved_one)
    inverse_diagonal_first = (
        diag_one + block_totals(jnp.stack([block_inner(masked_one, solved_one)]))[0]
    )
    rows_all, link_all, diagonal_blocks_full = (
        lax.all_gather(masked_two, "col", axis=1, tiled=True),
        lax.all_gather(lower_parent, "col", axis=1, tiled=True),
        lax.all_gather(inverse_diagonal_first, "col", axis=1, tiled=True),
    )
    local_ids = col_index * col_one + jnp.arange(col_one, dtype=jnp.int32)
    pick_all = (parent_two[None, :] == local_ids[:, None]).astype(jnp.float32)
    parent_cols = jnp.einsum(
        "ikb,km->imb",
        inverse_off_one.reshape(rows_here, col_one, BLOCK_SIDE),
        pick_all,
        precision=PRECISION_MODE,
    )
    direct = broadcast_product(root_inverse, masked_two)
    direct = direct + jnp.einsum(
        "imb,bme->ime",
        parent_cols,
        link_all.reshape(BLOCK_SIDE, super_two, BLOCK_SIDE),
        precision=PRECISION_MODE,
    ).reshape(rows_here, super_two * BLOCK_SIDE)
    across_all = jnp.einsum(
        "imb,ime->bme",
        parent_cols,
        rows_all.reshape(rows_here, super_two, BLOCK_SIDE),
        precision=PRECISION_MODE,
    ).reshape(BLOCK_SIDE, super_two * BLOCK_SIDE)
    summed = column_sums(jnp.concatenate([direct, across_all], axis=0))
    solved_two = summed[:rows_here]
    across_part = summed[rows_here:]
    totals = block_totals(jnp.stack([block_inner(masked_two, solved_two), across_part]))
    parent_diagonal = jnp.einsum(
        "vfl,fo->vol",
        diagonal_blocks_full.reshape(BLOCK_SIDE, first_supernodes, BLOCK_SIDE),
        select_owned_blocks,
        precision=PRECISION_MODE,
    )
    across = totals[1].reshape(BLOCK_SIDE, col_two, BLOCK_SIDE) + jnp.einsum(
        "bmd,dme->bme", parent_diagonal, link_own, precision=PRECISION_MODE
    )
    inverse_diag_two = (
        diag_two
        + totals[0]
        + jnp.einsum("dmb,dme->bme", link_own, across, precision=PRECISION_MODE).reshape(
            BLOCK_SIDE, col_two * BLOCK_SIDE
        )
    )
    return (
        inverse_off_one,
        inverse_diagonal_first,
        -(mask_two * solved_two),
        -across.reshape(BLOCK_SIDE, col_two * BLOCK_SIDE),
        inverse_diag_two,
    )


def solution(mesh):
    return jax.shard_map(
        local,
        mesh=mesh,
        in_specs=(
            P(("pole", "row"), "col"),
            P(("pole", "row"), "col"),
            P(),
            P("pole", "col"),
            P(("pole", "row"), "col"),
            P(),
            P(),
            P("pole", "col"),
            P("pole", "col"),
        ),
        out_specs=(
            P(("pole", "row"), "col"),
            P("pole", "col"),
            P(("pole", "row"), "col"),
            P("pole", "col"),
            P("pole", "col"),
        ),
        check_vma=False,
    )
```

profile of v0, /device:TPU:0, one launch (start us, length us, event | category | flops | bytes accessed | tf_op | source)
XLA Modules:
  0.0 674.7 jit_solution(6529609036820438768)
XLA Ops:
  7.2 0.0 all-gather.4.cloned.1.call-start
  7.2 1.6 copy.31
  8.8 0.8 convert_bitcast_fusion
  9.6 0.1 broadcast_bitcast_fusion
  9.6 0.1 broadcast_multiply_fusion
  9.7 1.0 copy-done.3
  10.7 31.8 %all_to_all.64 = f32[2048,4,32]{0,2,1:T(8,128)S(1)} all-to-all(f32[2048,4,32]{0,2,1:T(8,128)S(1)} %bitcast.119), channel_id=1, replica_groups=mesh['pole'=2,'row'=4,'col'=4] {'row'}, dimensions={1} | all-to-all | bytes 2097152 | tf_op jit(solution)/shard_map/all_to_all | solution.py:56
  42.5 17.6 %all_to_all.65 = f32[4,2048,32]{1,2,0:T(8,128)} all-to-all(f32[4,2048,32]{1,2,0:T(8,128)S(1)} %bitcast.127), channel_id=1, replica_groups=mesh['pole'=2,'row'=4,'col'=4] {'col'}, dimensions={0} | all-to-all | bytes 2097152 | tf_op jit(solution)/shard_map/all_to_all | solution.py:55
  60.1 0.0 all-gather.4.cloned.1.call-update
  60.2 0.0 reduce-scatter.3.cloned.1.call-start
  60.2 79.1 %all-gather.4.cloned.1.call-done = f32[2048,512]{0,1:T(8,128)} async-done(((f32[2048,128]{0,1:T(8,128)}), f32[2048,512]{0,1:T(8,128)}) %all-gather.4.cloned.1.call-update) | async-done | bytes 4194320 | tf_op jit(solution)/shard_map/all_gather | solution.py:62
  139.3 31.7 %fusion.26 = f32[512,2048]{1,0:T(8,128)S(1)} fusion(f32[2048,512]{0,1:T(8,128)} %all-gather.4.cloned.1.call-done, f32[2048,2048]{1,0:T(8,128)} %param.9), kind=kOutput, calls=%fused_computation.41 | convolution fusion | flops 25769803776 | bytes 25165824 | tf_op jit(solution)/shard_map/dot_general | solution.py:21
  170.9 2.2 copy.32
  173.2 0.0 reduce-scatter.3.cloned.1.call-update
  173.2 0.0 all-gather.8.cloned.1.call-start
  173.2 1.9 copy.34
  175.2 0.8 dynamic-slice_convert_fusion
  175.9 0.2 broadcast_in_dim.25
  176.2 1.3 copy-done.1
  177.5 2.4 bitcast_multiply_fusion.1
  179.9 0.0 all-gather.8.cloned.1.call-update
  179.9 0.0 all-gather.6.cloned.1.call-start
  179.9 52.1 %all_to_all.66 = f32[2048,4,64]{0,2,1:T(8,128)S(1)} all-to-all(f32[2048,4,64]{0,2,1:T(8,128)} %bitcast.114), channel_id=1, replica_groups=mesh['pole'=2,'row'=4,'col'=4] {'row'}, dimensions={1} | all-to-all | bytes 4194304 | tf_op jit(solution)/shard_map/all_to_all | solution.py:56
  232.1 51.7 %all_to_all.67 = f32[4,2048,64]{1,2,0:T(8,128)} all-to-all(f32[4,2048,64]{1,2,0:T(8,128)S(1)} %bitcast.123), channel_id=1, replica_groups=mesh['pole'=2,'row'=4,'col'=4] {'col'}, dimensions={0} | all-to-all | bytes 4194304 | tf_op jit(solution)/shard_map/all_to_all | solution.py:55
  283.8 0.0 all-gather.6.cloned.1.call-update
  283.8 0.0 reduce-scatter.5.cloned.1.call-start
  283.9 10.4 %all_gather.17 = f32[128,1024]{1,0:T(8,128)S(1)} all-gather(f32[128,256]{1,0:T(8,128)S(1)} %copy-done.5), channel_id=1, replica_groups=mesh['pole'=2,'row'=4,'col'=4] {'col'}, dimensions={1}, use_global_device_ids=true | all-gather | bytes 655360 | tf_op jit(solution)/shard_map/all_gather | solution.py:108
  294.2 0.2 copy.37
  294.5 0.0 reduce-scatter.3.cloned.1.call-done
  294.5 1.3 multiply_negate_fusion
  295.8 0.3 copy.42
  296.2 10.4 %fusion.2 = f32[8,2048,128]{1,2,0:T(8,128)} fusion(f32[128,8,128]{0,2,1:T(8,128)S(1)} %bitcast.129, f32[2048,128]{1,0:T(8,128)S(1)} %copy.42, f32[8]{0:T(128)S(1)} %compare_convert_fusion), kind=kOutput, calls=%fused_computation.4 | convolution fusion | flops 3223322624 | bytes 9961504 | tf_op jit(solution)/shard_map/imb,bme->ime/dot_general | solution.py:120
  306.5 11.1 %fusion = f32[8,128,128]{2,1,0:T(8,128)S(1)} fusion(f32[2048,8,128]{0,2,1:T(8,128)} %bitcast.120, f32[2048,128]{1,0:T(8,128)S(1)} %copy.42, f32[8]{0:T(128)S(1)} %compare_convert_fusion), kind=kOutput, calls=%fused_computation.2 | convolution fusion | flops 3223322624 | bytes 9961504 | tf_op jit(solution)/shard_map/imb,ime->bme/dot_general | solution.py:126
  317.7 135.8 %all-gather.6.cloned.1.call-done = f32[2048,1024]{0,1:T(8,128)} async-done(((f32[2048,256]{0,1:T(8,128)}), f32[2048,1024]{0,1:T(8,128)}) %all-gather.6.cloned.1.call-update) | async-done | bytes 8388624 | tf_op jit(solution)/shard_map/all_gather | solution.py:62
  453.4 60.5 %fusion.27 = f32[1024,2048]{1,0:T(8,128)S(1)} fusion(f32[2048,1024]{0,1:T(8,128)} %all-gather.6.cloned.1.call-done, f32[2048,2048]{1,0:T(8,128)} %param.9), kind=kOutput, calls=%fused_computation.42 | convolution fusion | flops 51539607552 | bytes 33554432 | tf_op jit(solution)/shard_map/dot_general | solution.py:21
  513.9 3.9 copy.35
  517.8 11.8 %bitcast_add_fusion = f32[2048,1024]{0,1:T(8,128)} fusion(f32[8,2048,128]{1,2,0:T(8,128)} %fusion.2, f32[2048,4,4,64]{0,3,1,2:T(8,128)} %copy.35), kind=kLoop, calls=%fused_computation.1 | loop fusion | flops 2097152 | bytes 25165824 | tf_op jit(solution)/shard_map/add | solution.py:120
  529.5 7.6 %pad_maximum_fusion = f32[2176,1024]{0,1:T(8,128)} fusion(f32[128,1024]{0,1:T(8,128)S(1)} %bitcast.128, f32[2048,1024]{0,1:T(8,128)} %bitcast_add_fusion), kind=kLoop, calls=%fused_computation | loop fusion | flops 2228224 | bytes 17825792 | tf_op jit(solution)/shard_map/concatenate | solution.py:132
  537.1 0.0 reduce-scatter.5.cloned.1.call-update
  537.1 0.0 all-reduce.3.cloned.1.call-start
  537.2 1.1 copy-done.4
  538.3 2.9 convolution_bitcast_fusion.1
  541.2 69.4 %reduce-scatter.5.cloned.1.call-done = f32[2176,256]{0,1:T(8,128)} async-done(((f32[2176,1024]{0,1:T(8,128)}), f32[2176,256]{0,1:T(8,128)}) %reduce-scatter.5.cloned.1.call-update) | async-done | bytes 2228240 | tf_op jit(solution)/shard_map/reduce_scatter | solution.py:43
  610.5 4.7 fusion.10
  615.2 2.0 fusion.28
  617.3 0.9 slice_bitcast_fusion.1
  618.2 0.7 pad_maximum_fusion.1
  618.9 0.0 all-reduce.3.cloned.1.call-update
  619.0 0.1 dynamic_slice.13
  619.0 0.1 copy.33
  619.1 0.1 copy.40
  619.2 2.9 copy.44
  622.1 33.3 %all-reduce.3.cloned.1.call-done = (f32[128,128]{0,1:T(8,128)}, f32[2,128,256]{1,2,0:T(8,128)}) async-done(((f32[128,128]{0,1:T(8,128)}, f32[2,128,256]{1,2,0:T(8,128)}), (f32[128,128]{0,1:T(8,128)}, f32[2,128,256]{1,2,0:T(8,128)})) %all-reduce.3.cloned.1.call-update) | async-done | bytes 327696 | tf_op jit(solution)/shard_map/psum | solution.py:47
  655.5 0.8 add.40
  656.3 0.7 copy.43
  657.0 5.8 all_gather.19
  662.8 0.9 slice.18
  663.7 0.1 copy.48
  663.9 0.4 fusion.22
  664.3 0.4 fusion.25
  664.7 0.8 copy.45
  665.5 0.3 fusion.13
  665.7 0.9 fusion.16
  666.7 0.8 copy.46
  (17 shorter events, 0.0 us)
Async XLA Ops:
  7.2 132.1 %all-gather.4.cloned.1.call-start = ((), (), s32[]{:S(2)}) async-start(), calls=%async_computation.6 | async-start | bytes 5242880 | tf_op jit(solution)/shard_map/all_gather | solution.py:62
  9.7 1.0 copy-start.3
  60.2 234.3 %reduce-scatter.3.cloned.1.call-start = ((), (), s32[]{:S(2)}) async-start(), calls=%async_computation.7 | async-start | bytes 5242880 | tf_op jit(solution)/shard_map/reduce_scatter | solution.py:43
  173.2 133.4 %all-gather.8.cloned.1.call-start = ((), (), s32[]{:S(2)}) async-start(), calls=%async_computation.9 | async-start | bytes 10485760 | tf_op jit(solution)/shard_map/all_gather | solution.py:107
  176.2 1.3 copy-start.1
  177.5 106.4 %copy-start.5 = (f32[128,256]{1,0:T(8,128)S(1)}, f32[128,256]{1,0:T(8,128)}, u32[]{:S(2)}) copy-start(f32[128,256]{1,0:T(8,128)} %param.16) | copy-start | bytes 393220
  179.9 114.6 %copy-start.8 = (s32[8]{0:T(128)S(1)}, s32[8]{0:T(128)}, u32[]{:S(2)}) copy-start(s32[8]{0:T(128)} %param.15) | copy-start | bytes 100
  179.9 273.5 %all-gather.6.cloned.1.call-start = ((), (), s32[]{:S(2)}) async-start(), calls=%async_computation.8 | async-start | bytes 10485760 | tf_op jit(solution)/shard_map/all_gather | solution.py:62
  283.8 326.7 %reduce-scatter.5.cloned.1.call-start = ((), (), s32[]{:S(2)}) async-start(), calls=%async_computation.10 | async-start | bytes 11141120 | tf_op jit(solution)/shard_map/reduce_scatter | solution.py:43
  296.2 21.5 %copy-start.2 = (f32[2048,128]{1,0:T(8,128)}, f32[2048,128]{1,0:T(8,128)S(1)}, u32[]{:S(2)}) copy-start(f32[2048,128]{1,0:T(8,128)S(1)} %copy.42) | copy-start | bytes 3145732
  537.1 1.2 copy-start.4
  537.1 78.2 %copy-start = (f32[2048,256]{0,1:T(8,128)S(1)}, f32[2048,256]{0,1:T(8,128)}, u32[]{:S(2)}) copy-start(f32[2048,256]{0,1:T(8,128)} %bitcast_multiply_fusion.1) | copy-start | bytes 6291460
  537.1 81.9 %copy-start.7 = (f32[128,128]{1,0:T(8,128)S(1)}, f32[128,128]{1,0:T(8,128)}, u32[]{:S(2)}) copy-start(f32[128,128]{1,0:T(8,128)} %param.12) | copy-start | bytes 196612
  537.1 82.0 %copy-start.6 = (f32[128,256]{1,0:T(8,128)S(1)}, f32[128,256]{1,0:T(8,128)}, u32[]{:S(2)}) copy-start(f32[128,256]{1,0:T(8,128)} %param.17) | copy-start | bytes 393220
  537.1 118.3 %all-reduce.3.cloned.1.call-start = ((), (), s32[]{:S(2)}) async-start(), calls=%async_computation.11 | async-start | bytes 655360 | tf_op jit(solution)/shard_map/psum | solution.py:47
Sparse Core Ops, SparseCore 0:
  60.3 78.9 all-gather.3
  173.3 43.0 reduce-scatter.2
  218.6 83.5 all-gather.7
  303.7 149.6 all-gather.5
  537.2 73.2 reduce-scatter.4
  619.1 36.3 all-reduce.2
where the time goes:
time: 683 us; the launch traced here: 675 us
  waiting for transfers between devices  318 us (47%)
  blocking collectives  169 us (25%)
  matrix products  120 us (18%)
  other arithmetic  31.8 us (5%)
  local copies, waits for them, and re-layouts  21.2 us (3%)
  between operations  14.8 us (2%)
    all_gather x2, waiting for transfers between devices, broadcast_product(): lax.all_gather(swapped, 'row', axis=1, tiled=True)  215 us
    dot_general x2, matrix products, product(): jnp.dot(left_part, right_part, precision=PRECISION_MODE, preferred_elemen...  92.1 us
    all_to_all x2, blocking collectives, broadcast_product(): lax.all_to_all(masked, 'row', split_axis=1, concat_axis=0, tiled=True)  83.9 us
    reduce_scatter x2, waiting for transfers between devices, column_sums(): return lax.psum_scatter(partial_sum, 'col', scatter_dimension=1, tiled=True)  69.4 us
    all_to_all x2, blocking collectives, broadcast_product(): lax.all_to_all(lax.all_to_all(masked, 'row', split_axis=1, concat_axis=0,...  69.3 us
    psum x1, waiting for transfers between devices, block_totals(): return lax.psum(stacked, 'row')  33.3 us
  transfers between devices with their start and end apart: 6, of which 4 were waited for; matrix products, arithmetic and copies ran while one was open for 5% of the time, Pallas kernels for 0%

commit v1 on v0

v1 whole, which is shorter than its diff:
```python
import functools

import jax
import jax.numpy as jnp
from jax import lax
from jax.experimental import pallas as pl
from jax.experimental.pallas import tpu as pltpu
from jax.sharding import PartitionSpec as P

BLOCK_SIDE = 128
MODE = lax.Precision.HIGH


def product(left_part, right_part):
    return jnp.dot(left_part, right_part, precision=MODE, preferred_element_type=jnp.float32)


def transposed_product(left_part, right_part):
    return lax.dot_general(
        left_part,
        right_part,
        (((0,), (0,)), ((), ())),
        precision=MODE,
        preferred_element_type=jnp.float32,
    )


def pack_kernel(count, blocks_one, blocks_two, order_ref, one_ref, two_ref, out_ref, sem):
    blocks = blocks_one + blocks_two

    @pl.loop(0, count)
    def _(slot):
        tile = order_ref[slot]
        row = lax.div(tile, blocks) * BLOCK_SIDE
        block = lax.rem(tile, blocks)
        rows = pl.ds(pl.multiple_of(row, BLOCK_SIDE), BLOCK_SIDE)

        @pl.when(block < blocks_one)
        def _():
            cols = pl.ds(pl.multiple_of(block * BLOCK_SIDE, BLOCK_SIDE), BLOCK_SIDE)
            pltpu.make_async_copy(one_ref.at[rows, cols], out_ref.at[slot], sem).start()

        @pl.when(block >= blocks_one)
        def _():
            cols = pl.ds(
                pl.multiple_of((block - blocks_one) * BLOCK_SIDE, BLOCK_SIDE), BLOCK_SIDE
            )
            pltpu.make_async_copy(two_ref.at[rows, cols], out_ref.at[slot], sem).start()

    pltpu.make_async_copy(out_ref, out_ref, sem).wait()


def pack_pair(order, one, two):
    count = order.shape[0]
    return pl.pallas_call(
        functools.partial(
            pack_kernel, count, one.shape[1] // BLOCK_SIDE, two.shape[1] // BLOCK_SIDE
        ),
        out_shape=jax.ShapeDtypeStruct((count, BLOCK_SIDE, BLOCK_SIDE), jnp.float32),
        in_specs=[
            pl.BlockSpec(memory_space=pltpu.SMEM),
            pl.BlockSpec(memory_space=pl.ANY),
            pl.BlockSpec(memory_space=pl.ANY),
        ],
        out_specs=pl.BlockSpec(memory_space=pl.ANY),
        scratch_shapes=[pltpu.SemaphoreType.DMA],
        name="pack_pair",
    )(order, one, two)


def pick_kernel(count, blocks, order_ref, dense_ref, out_ref, sem):
    @pl.loop(0, count)
    def _(slot):
        tile = order_ref[slot]
        rows = pl.ds(
            pl.multiple_of(lax.div(tile, blocks) * BLOCK_SIDE, BLOCK_SIDE), BLOCK_SIDE
        )
        cols = pl.ds(
            pl.multiple_of(lax.rem(tile, blocks) * BLOCK_SIDE, BLOCK_SIDE), BLOCK_SIDE
        )
        pltpu.make_async_copy(dense_ref.at[rows, cols], out_ref.at[slot], sem).start()

    pltpu.make_async_copy(out_ref, out_ref, sem).wait()


def pick_tiles(order, dense):
    count = order.shape[0]
    return pl.pallas_call(
        functools.partial(pick_kernel, count, dense.shape[1] // BLOCK_SIDE),
        out_shape=jax.ShapeDtypeStruct((count, BLOCK_SIDE, BLOCK_SIDE), jnp.float32),
        in_specs=[
            pl.BlockSpec(memory_space=pltpu.SMEM),
            pl.BlockSpec(memory_space=pl.ANY),
        ],
        out_specs=pl.BlockSpec(memory_space=pl.ANY),
        scratch_shapes=[pltpu.SemaphoreType.DMA],
        name="pick_tiles",
    )(order, dense)


def spread_kernel(count, blocks, place_ref, packed_ref, out_ref, zeros, sem):
    zeros[...] = jnp.zeros_like(zeros)

    @pl.loop(0, count)
    def _(tile):
        place = place_ref[tile]
        rows = pl.ds(
            pl.multiple_of(lax.div(tile, blocks) * BLOCK_SIDE, BLOCK_SIDE), BLOCK_SIDE
        )
        cols = pl.ds(
            pl.multiple_of(lax.rem(tile, blocks) * BLOCK_SIDE, BLOCK_SIDE), BLOCK_SIDE
        )

        @pl.when(place >= 0)
        def _():
            pltpu.make_async_copy(packed_ref.at[place], out_ref.at[rows, cols], sem).start()

        @pl.when(place < 0)
        def _():
            pltpu.make_async_copy(zeros, out_ref.at[rows, cols], sem).start()

    pltpu.make_async_copy(out_ref, out_ref, sem).wait()


def spread_tiles(place, packed, blocks):
    count = place.shape[0]
    return pl.pallas_call(
        functools.partial(spread_kernel, count, blocks),
        out_shape=jax.ShapeDtypeStruct(
            (count // blocks * BLOCK_SIDE, blocks * BLOCK_SIDE), jnp.float32
        ),
        in_specs=[
            pl.BlockSpec(memory_space=pltpu.SMEM),
            pl.BlockSpec(memory_space=pl.ANY),
        ],
        out_specs=pl.BlockSpec(memory_space=pl.ANY),
        scratch_shapes=[
            pltpu.VMEM((BLOCK_SIDE, BLOCK_SIDE), jnp.float32),
            pltpu.SemaphoreType.DMA,
        ],
        name="spread_tiles",
    )(place, packed)


def expand_blocks(pattern):
    count_rows, count_cols = pattern.shape
    spread = jnp.broadcast_to(
        pattern.astype(jnp.float32)[:, None, :, None],
        (count_rows, BLOCK_SIDE, count_cols, BLOCK_SIDE),
    )
    return spread.reshape(count_rows * BLOCK_SIDE, count_cols * BLOCK_SIDE)


def gather_plane(packed):
    ranks_col = lax.axis_size("col")
    whole = lax.all_gather(packed, "row", axis=0)
    swapped = lax.all_to_all(whole, "col", split_axis=0, concat_axis=0, tiled=True)
    return swapped.reshape((ranks_col, -1) + packed.shape)


def capacity_levels(total):
    if total < 16:
        return (total,)
    return tuple(sorted({-(-total * part // 24) for part in (10, 11, 12, 13, 14, 16, 24)}))


def with_capacity(
    capacity,
    tables,
    root_inverse,
    lower_one,
    diag_one,
    lower_two,
    parent_two,
    lower_parent,
    diag_two,
):
    order, rank, pattern = tables
    ranks_row, ranks_col, total = order.shape
    row, col = lax.axis_index("row"), lax.axis_index("col")
    rows_here, cols_here = root_inverse.shape
    row_blocks = rows_here // BLOCK_SIDE
    col_one, col_two = (
        lower_one.shape[1] // BLOCK_SIDE,
        lower_two.shape[1] // BLOCK_SIDE,
    )
    blocks = col_one + col_two
    share = ranks_row // ranks_col

    own = lax.dynamic_index_in_dim(
        lax.dynamic_index_in_dim(order, row, 0, False), col, 0, False
    )[:capacity]
    packed = pack_pair(own, lower_one, lower_two)
    plane = gather_plane(packed)

    here = lax.dynamic_slice_in_dim(rank, col * share, share, 0)
    base = (
        jnp.arange(ranks_col)[None, :, None] * share + jnp.arange(share)[:, None, None]
    ) * capacity
    place = jnp.where(here >= 0, here + base, -1).reshape(share, ranks_col, row_blocks, blocks)
    place = place.transpose(0, 2, 1, 3).reshape(-1)
    right = spread_tiles(
        place.astype(jnp.int32),
        plane.reshape(-1, BLOCK_SIDE, BLOCK_SIDE),
        ranks_col * blocks,
    )
    partial_sum = product(root_inverse, right)

    outs = lax.dynamic_index_in_dim(order, row, 0, False)[:, :capacity]
    tiles = (
        lax.div(outs, blocks) * (ranks_col * blocks)
        + jnp.arange(ranks_col, dtype=jnp.int32)[:, None] * blocks
        + lax.rem(outs, blocks)
    )
    chosen = pick_tiles(tiles.reshape(-1), partial_sum)
    summed = lax.psum_scatter(chosen, "col", scatter_dimension=0, tiled=True)

    own_rank = lax.dynamic_index_in_dim(
        lax.dynamic_index_in_dim(rank, row, 0, False), col, 0, False
    )
    own_rank = own_rank.reshape(row_blocks, blocks)
    solved_one = spread_tiles(own_rank[:, :col_one].reshape(-1), summed, col_one)
    direct = spread_tiles(own_rank[:, col_one:].reshape(-1), summed, col_two)

    own_pattern = lax.dynamic_index_in_dim(
        lax.dynamic_index_in_dim(pattern, row, 0, False), col, 0, False
    ).reshape(row_blocks, blocks)
    mask_one = expand_blocks(own_pattern[:, :col_one])
    mask_two = expand_blocks(own_pattern[:, col_one:])
    masked_one = lower_one * mask_one
    masked_two = lower_two * mask_two

    def part(array, index):
        return lax.slice_in_dim(array, index * BLOCK_SIDE, (index + 1) * BLOCK_SIDE, axis=1)

    inverse_off_one = -solved_one
    columns = lax.all_gather(inverse_off_one, "col", axis=1, tiled=True)
    inner_one = jnp.concatenate(
        [transposed_product(part(masked_one, k), part(solved_one, k)) for k in range(col_one)],
        axis=1,
    )
    inverse_diagonal_first = diag_one + lax.psum(inner_one, "row")
    diagonals = lax.all_gather(inverse_diagonal_first, "col", axis=1, tiled=True)

    owned_parent = lax.dynamic_slice_in_dim(parent_two, col * col_two, col_two, 0)
    solved, inner_two, across_part, parent_diagonals = [], [], [], []
    for m in range(col_two):
        start = owned_parent[m] * BLOCK_SIDE
        parent_cols = lax.dynamic_slice_in_dim(columns, start, BLOCK_SIDE, 1)
        parent_diagonals.append(lax.dynamic_slice_in_dim(diagonals, start, BLOCK_SIDE, 1))
        solved_m = part(direct, m) + product(parent_cols, part(lower_parent, m))
        solved.append(solved_m)
        inner_two.append(transposed_product(part(masked_two, m), solved_m))
        across_part.append(transposed_product(parent_cols, part(masked_two, m)))
    totals = lax.psum(jnp.concatenate(inner_two + across_part, axis=1), "row")
    across, diag = [], []
    for m in range(col_two):
        link = part(lower_parent, m)
        across_m = part(totals, col_two + m) + product(parent_diagonals[m], link)
        across.append(across_m)
        diag.append(part(diag_two, m) + part(totals, m) + transposed_product(link, across_m))
    return (
        inverse_off_one,
        inverse_diagonal_first,
        -(mask_two * jnp.concatenate(solved, axis=1)),
        -jnp.concatenate(across, axis=1),
        jnp.concatenate(diag, axis=1),
    )


def local(
    root_inverse,
    lower_one,
    pattern_one,
    diag_one,
    lower_two,
    pattern_two,
    parent_two,
    lower_parent,
    diag_two,
):
    ranks_row, ranks_col = lax.axis_size("row"), lax.axis_size("col")
    row_blocks = root_inverse.shape[0] // BLOCK_SIDE
    pattern = jnp.concatenate(
        [
            pattern_one.reshape(ranks_row, row_blocks, ranks_col, -1),
            pattern_two.reshape(ranks_row, row_blocks, ranks_col, -1),
        ],
        axis=3,
    )
    pattern = pattern.transpose(0, 2, 1, 3).reshape(ranks_row, ranks_col, -1).astype(jnp.int32)
    total = pattern.shape[2]
    running = jnp.cumsum(pattern, axis=2)
    counts = running[:, :, -1:]
    rank = jnp.where(pattern > 0, running - 1, -1)
    slot = jnp.where(pattern > 0, running - 1, counts + jnp.arange(total) - running)
    order = jnp.sum(
        jnp.where(
            slot[:, :, None, :] == jnp.arange(total)[:, None],
            jnp.arange(total, dtype=jnp.int32),
            0,
        ),
        axis=3,
        dtype=jnp.int32,
    )
    levels = capacity_levels(total)
    operands = (
        (order, rank.astype(jnp.int32), pattern),
        root_inverse,
        lower_one,
        diag_one,
        lower_two,
        parent_two,
        lower_parent,
        diag_two,
    )
    branches = [functools.partial(with_capacity, level) for level in levels]
    if len(branches) == 1:
        return branches[0](*operands)
    index = jnp.sum(jnp.max(counts) > jnp.array(levels[:-1])).astype(jnp.int32)
    return lax.switch(index, branches, *operands)


def solution(mesh):
    return jax.shard_map(
        local,
        mesh=mesh,
        in_specs=(
            P(("pole", "row"), "col"),
            P(("pole", "row"), "col"),
            P(),
            P("pole", "col"),
            P(("pole", "row"), "col"),
            P(),
            P(),
            P("pole", "col"),
            P("pole", "col"),
        ),
        out_specs=(
            P(("pole", "row"), "col"),
            P("pole", "col"),
            P(("pole", "row"), "col"),
            P("pole", "col"),
            P("pole", "col"),
        ),
        check_vma=False,
    )
```

time: 683 us -> 842 us (1.23)
  Pallas kernels: 0 us -> 385 us
  blocking collectives: 169 us -> 5.79 us
  matrix products: 120 us -> 63 us
  loops' own time: 0 us -> 33.2 us
  other arithmetic: 31.8 us -> 9.88 us
  local copies, waits for them, and re-layouts: 21.2 us -> 8.6 us
  waiting for transfers between devices: 318 us -> 306 us
    pallas_call x0 -> x5, Pallas kernels: none -> 385 us  [the longest x1 176 us: pick_tiles(): pl.pallas_call(functools.partial(pick_kernel, count, dense.shape[1] // BL...]
    all_to_all x4 -> x0, blocking collectives: 153 us -> none  [the longest x2 83.9 us: broadcast_product(): lax.all_to_all(masked, 'row', split_axis=1, concat_axis=0, tiled=True)]
    all_gather x3 -> x2, waiting for transfers between devices: 215 us -> 122 us  [the longest x1 110 us: gather_plane(): whole = lax.all_gather(packed, 'row', axis=0)]
    all_to_all x0 -> x1, waiting for transfers between devices: none -> 63.4 us  [gather_plane(): lax.all_to_all(whole, 'col', split_axis=0, concat_axis=0, tiled=True)]
    dot_general x9 -> x12, matrix products: 120 us -> 63 us  [the longest x5 54.9 us: product(): jnp.dot(left_part, right_part, precision=MODE, preferred_element_type=jnp...]
    another operation x0 -> x1, loops' own time: none -> 33.2 us  [local(): return lax.switch(index, branches, *operands)]
    reduce_scatter x2 -> x1, waiting for transfers between devices: 69.4 us -> 84.5 us  [with_capacity(): summed = lax.psum_scatter(chosen, 'col', scatter_dimension=0, tiled=True)]
    add x3 -> x2, other arithmetic: 13.5 us -> 0.92 us  [the longest x1 0.85 us: with_capacity(): inverse_diagonal_first = diag_one + lax.psum(inner_one, 'row')]
  transfers between devices with their start and end apart: 6 -> 5, of which waited for: 4 -> 5; matrix products, arithmetic and copies ran while one was open for 5% -> 1% of each run, Pallas kernels for 0% -> 3%
where the time goes in v1:
time: 842 us; the launch traced here: 832 us
  Pallas kernels  385 us (46%)
  waiting for transfers between devices  306 us (36%)
  matrix products  63 us (7%)
  loops' own time  33.2 us (4%)
  between operations  14.9 us (2%)
  other arithmetic  9.88 us (1%)
  local copies, waits for them, and re-layouts  8.6 us (1%)
    pallas_call x1, Pallas kernels, pick_tiles(): pl.pallas_call(functools.partial(pick_kernel, count, dense.shape[1] // BL...  176 us
    pallas_call x3, Pallas kernels, spread_tiles(): pl.pallas_call(functools.partial(spread_kernel, count, blocks), out_shape...  163 us
    all_gather x1, waiting for transfers between devices, gather_plane(): whole = lax.all_gather(packed, 'row', axis=0)  110 us
    reduce_scatter x1, waiting for transfers between devices, with_capacity(): summed = lax.psum_scatter(chosen, 'col', scatter_dimension=0, tiled=True)  84.5 us
    all_to_all x1, waiting for transfers between devices, gather_plane(): lax.all_to_all(whole, 'col', split_axis=0, concat_axis=0, tiled=True)  63.4 us
    dot_general x5, matrix products, product(): jnp.dot(left_part, right_part, precision=MODE, preferred_element_type=jnp...  54.9 us
    pallas_call x1, Pallas kernels, pack_pair(): pl.pallas_call(functools.partial(pack_kernel, count, one.shape[1] // BLOC...  45.5 us
    psum x1, waiting for transfers between devices, with_capacity(): inverse_diagonal_first = diag_one + lax.psum(inner_one, 'row')  36.4 us
  transfers between devices with their start and end apart: 5, of which 5 were waited for; matrix products, arithmetic and copies ran while one was open for 1% of the time, Pallas kernels for 3%

profile of v1, /device:TPU:0, one launch (start us, length us, event | category | flops | bytes accessed | tf_op | source)
XLA Modules:
  0.0 831.8 jit_solution(1489751278557092820)
XLA Ops:
  7.2 0.8 reshape.444
  7.9 0.8 reshape.443
  8.7 0.2 copy.259
  8.9 0.1 reshape.445
  9.0 0.9 reduce_window_sum.11
  9.9 0.7 fusion.268
  10.6 1.9 fusion.260
  13.3 811.5 %conditional.1 = (f32[2048,128]{1,0:T(8,128)}, f32[128,128]{1,0:T(8,128)}, f32[2048,256]{1,0:T(8,128)}, f32[128,256]{1,0:T(8,128)}, f32[128,256]{1,0:T(8,128)}) conditional(s32[]{:T(128)} %clamp.129, (s32[4,4,48]{2,1,0:T(4,128)S(1)}, s32[]{:T(128)}, f32[2048,128]{1,0:T(8,128)}, f32[2048,256]{1,0:T(8,128)}, ...), branch_computations={%region_4.8_spmd, %region_8.12_spmd, %region_12.16_spmd, %region_1... | conditional | flops 40118079488 | bytes 271091040 | solution.py:321
  22.1 0.0 all-gather.28.cloned.1.call-start
  22.2 0.1 copy.263
  22.3 0.1 fusion.64
  22.4 0.4 select_reduce_fusion.1
  22.8 0.5 slice_bitcast_fusion.1.order_ref
  23.3 45.5 %pack_pair.8 = f32[22,128,128]{2,1,0:T(8,128)} custom-call(s32[22]{0:T(128)} %slice_bitcast_fusion.1.order_ref, f32[2048,128]{1,0:T(8,128)} %get-tuple-element.326.one_ref, f32[2048,256]{1,0:T(8,128)} %get-tuple-element.333.two_ref), custom_call_target="tpu_custom_call" | custom-call | tf_op jit(solution)/shard_map/cond/branch_1_fun/pack_pair/pallas_call | solution.py:55
  68.8 109.6 %all-gather.28.cloned.1.call-done = f32[88,128,128]{2,1,0:T(8,128)} async-done(((f32[22,128,128]{2,1,0:T(8,128)}), f32[88,128,128]{2,1,0:T(8,128)}) %all-gather.28.cloned.1.call-update) | async-done | bytes 5767184 | tf_op jit(solution)/shard_map/cond/branch_1_fun/all_gather | solution.py:156
  178.3 5.1 all-to-all-start.1
  183.5 0.0 reduce-scatter.10.cloned.1.call-start
  183.6 0.1 remainder_add_fusion.1
  183.6 0.6 reshape.389.order_ref
  184.2 0.1 add_select_fusion.3
  184.3 0.1 reshape.390
  184.4 0.7 reshape.391.place_ref
  185.1 63.4 %all-to-all-done.1 = f32[4,22,128,128]{3,2,1,0:T(8,128)} async-done(((f32[4,22,128,128]{3,2,1,0:T(8,128)}), f32[4,22,128,128]{3,2,1,0:T(8,128)}, u32[]{:S(2)}, u32[]{:S(2)}) %all-to-all-start.1) | async-done | bytes 5767200 | tf_op jit(solution)/shard_map/cond/branch_1_fun/all_to_all | solution.py:157
  248.6 123.4 %spread_tiles.24 = f32[2048,1536]{1,0:T(8,128)} custom-call(s32[192]{0:T(256)} %reshape.391.place_ref, f32[88,128,128]{2,1,0:T(8,128)} %bitcast.17.packed_ref), custom_call_target="tpu_custom_call" | custom-call | tf_op jit(solution)/shard_map/cond/branch_1_fun/spread_tiles/pallas_call | solution.py:127
  372.0 48.7 %convolution_bitcast_fusion.3.dense_ref = f32[2048,1536]{1,0:T(8,128)} fusion(f32[2048,1536]{1,0:T(8,128)} %spread_tiles.24, f32[2048,2048]{1,0:T(8,128)} %get-tuple-element.340), kind=kOutput, calls=%fused_computation.69 | convolution fusion | flops 38654705664 | bytes 41943040 | tf_op jit(solution)/shard_map/cond/branch_1_fun/dot_general | solution.py:15
  420.7 176.5 %pick_tiles.8 = f32[88,128,128]{2,1,0:T(8,128)} custom-call(s32[88]{0:T(128)} %reshape.389.order_ref, f32[2048,1536]{1,0:T(8,128)} %convolution_bitcast_fusion.3.dense_ref), custom_call_target="tpu_custom_call" | custom-call | tf_op jit(solution)/shard_map/cond/branch_1_fun/pick_tiles/pallas_call | solution.py:88
  597.2 0.3 all-gather.26.cloned.1.call-start
  597.4 0.1 reshape.387
  597.5 0.6 slice_reduce_fusion.1.place_ref
  598.2 84.5 %reduce-scatter.10.cloned.1.call-done.packed_ref = f32[22,128,128]{2,1,0:T(8,128)} async-done(((f32[88,128,128]{2,1,0:T(8,128)}), f32[22,128,128]{2,1,0:T(8,128)}) %reduce-scatter.10.cloned.1.call-update) | async-done | bytes 1441808 | tf_op jit(solution)/shard_map/cond/branch_1_fun/reduce_scatter | solution.py:216
  682.6 17.7 %spread_tiles.25 = f32[2048,128]{1,0:T(8,128)} custom-call(s32[16]{0:T(128)} %slice_reduce_fusion.1.place_ref, f32[22,128,128]{2,1,0:T(8,128)} %reduce-scatter.10.cloned.1.call-done.packed_ref), custom_call_target="tpu_custom_call" | custom-call | tf_op jit(solution)/shard_map/cond/branch_1_fun/spread_tiles/pallas_call | solution.py:127
  700.3 2.3 neg.45
  702.6 0.0 all-reduce.17.cloned.1.call-start
  702.7 0.1 slice.481
  702.8 0.1 dynamic_slice.178
  702.8 0.6 fusion.262
  704.7 0.1 reshape.393
  704.8 0.6 reshape.395.place_ref
  705.4 0.1 fusion.63
  705.6 0.1 broadcast_bitcast_fusion.1
  705.6 0.1 slice_convert_fusion.2
  705.7 21.8 %spread_tiles.26 = f32[2048,256]{1,0:T(8,128)} custom-call(s32[32]{0:T(128)} %reshape.395.place_ref, f32[22,128,128]{2,1,0:T(8,128)} %reduce-scatter.10.cloned.1.call-done.packed_ref), custom_call_target="tpu_custom_call" | custom-call | tf_op jit(solution)/shard_map/cond/branch_1_fun/spread_tiles/pallas_call | solution.py:127
  727.6 2.0 fusion.40
  729.5 12.2 %all-gather.26.cloned.1.call-done = f32[2048,512]{1,0:T(8,128)} async-done(((f32[2048,128]{1,0:T(8,128)}), f32[2048,512]{1,0:T(8,128)}) %all-gather.26.cloned.1.call-update) | async-done | bytes 4194320 | tf_op jit(solution)/shard_map/cond/branch_1_fun/all_gather | solution.py:237
  741.8 2.1 convolution_add_fusion.4
  743.9 2.0 convolution_add_fusion.5
  745.9 0.6 broadcast_in_dim.119
  746.5 1.7 fusion.37
  748.2 1.0 fusion.44
  749.2 1.0 fusion.48
  750.2 0.2 copy-done.50
  750.4 1.0 fusion.42
  751.4 1.0 fusion.46
  752.4 0.7 pad_maximum_fusion.2
  753.2 0.1 copy.262
  753.3 36.4 %all-reduce.17.cloned.1.call-done = (f32[128,128]{1,0:T(8,128)}, f32[128,512]{0,1:T(8,128)}) async-done(((f32[128,128]{1,0:T(8,128)}, f32[128,512]{0,1:T(8,128)}), (f32[128,128]{1,0:T(8,128)}, f32[128,512]{0,1:T(8,128)})) %all-reduce.17.cloned.1.call-update) | async-done | bytes 327696 | tf_op jit(solution)/shard_map/cond/branch_1_fun/psum | solution.py:242
  789.7 0.9 add.506
  790.5 5.8 all_gather.63
  796.3 1.1 convolution_add_fusion.6
  797.4 1.1 convolution_add_fusion.7
  798.5 1.0 fusion.38
  799.6 1.0 fusion.39
  800.6 0.8 copy.298
  801.4 0.8 copy.305
  (38 shorter events, 0.3 us)
Async XLA Ops:
  22.1 156.2 %all-gather.28.cloned.1.call-start = ((), (), s32[]{:S(2)}) async-start(), calls=%async_computation.20 | async-start | bytes 7208960 | tf_op jit(solution)/shard_map/cond/branch_1_fun/all_gather | solution.py:156
  178.3 70.2 %all-to-all-start.1 = ((f32[4,22,128,128]{3,2,1,0:T(8,128)}), f32[4,22,128,128]{3,2,1,0:T(8,128)}, u32[]{:S(2)}, u32[]{:S(2)}) async-start(f32[4,22,128,128]{3,2,1,0:T(8,128)} %bitcast.291), calls=%async_computation.2 | async-start | bytes 11534336 | tf_op jit(solution)/shard_map/cond/branch_1_fun/all_to_all | solution.py:157
  183.5 499.2 %reduce-scatter.10.cloned.1.call-start = ((), (), s32[]{:S(2)}) async-start(), calls=%async_computation.18 | async-start | bytes 7208960 | tf_op jit(solution)/shard_map/cond/branch_1_fun/reduce_scatter | solution.py:216
  597.2 144.6 %all-gather.26.cloned.1.call-start = ((), (), s32[]{:S(2)}) async-start(), calls=%async_computation.19 | async-start | bytes 5242880 | tf_op jit(solution)/shard_map/cond/branch_1_fun/all_gather | solution.py:237
  700.3 2.4 copy-start.64
  702.6 25.0 %copy-start.8 = (f32[2048,128]{1,0:T(8,128)S(1)}, f32[2048,128]{1,0:T(8,128)}, u32[]{:S(2)}) copy-start(f32[2048,128]{1,0:T(8,128)} %get-tuple-element.326.one_ref) | copy-start | bytes 3145732 | tf_op jit(solution)/shard_map/cond
  702.6 25.0 %copy-start.24 = (f32[2048,128]{1,0:T(8,128)S(1)}, f32[2048,128]{1,0:T(8,128)}, u32[]{:S(2)}) copy-start(f32[2048,128]{1,0:T(8,128)} %spread_tiles.25) | copy-start | bytes 3145732 | tf_op jit(solution)/shard_map/cond
  702.6 87.1 %all-reduce.17.cloned.1.call-start = ((), (), s32[]{:S(2)}) async-start(), calls=%async_computation.21 | async-start | bytes 655360 | tf_op jit(solution)/shard_map/cond/branch_1_fun/psum | solution.py:242
  705.7 36.1 %copy-start.15 = (f32[128,256]{1,0:T(8,128)S(1)}, f32[128,256]{1,0:T(8,128)}, u32[]{:S(2)}) copy-start(f32[128,256]{1,0:T(8,128)} %get-tuple-element.361) | copy-start | bytes 393220 | tf_op jit(solution)/shard_map/cond
  729.5 14.4 %copy-start.29 = (f32[2048,256]{1,0:T(8,128)S(1)}, f32[2048,256]{1,0:T(8,128)}, u32[]{:S(2)}) copy-start(f32[2048,256]{1,0:T(8,128)} %spread_tiles.26) | copy-start | bytes 6291460 | tf_op jit(solution)/shard_map/cond
  743.9 2.6 copy-start.1
  748.2 2.2 copy-start.50
  750.4 2.8 copy-start.36
  751.4 38.3 %copy-start.57 = (f32[128,128]{1,0:T(8,128)S(1)}, f32[128,128]{1,0:T(8,128)}, u32[]{:S(2)}) copy-start(f32[128,128]{1,0:T(8,128)} %get-tuple-element.347) | copy-start | bytes 196612 | tf_op jit(solution)/shard_map/cond
  790.5 11.6 %copy-start.43 = (f32[128,128]{1,0:T(8,128)}, f32[128,128]{1,0:T(8,128)S(1)}, u32[]{:S(2)}) copy-start(f32[128,128]{1,0:T(8,128)S(1)} %add.506) | copy-start | bytes 196612 | tf_op jit(solution)/shard_map/cond
Sparse Core Ops, SparseCore 0:
  68.9 109.3 all-gather.27
  597.3 85.2 reduce-scatter.9
  702.7 38.9 all-gather.25
  753.3 36.3 all-reduce.16
